TPU v7x, 256 devices: a whole 4x4x8 slice. The times are simulated.
256 devices in a mesh: seq: 64 (over x, z, core), tp: 4 (over y).
Axes of the slice: x: 4, y: 4, z: 8, core: 2. Of those that a mesh axis runs over, the one named last changes fastest.
Arguments:
- x_codes: bfloat16 [16384, 8192], P(('seq', 'tp')), may hold values from -4 to 4
- x_exps: int32 [16384, 64], P(('seq', 'tp')), may hold values from -2 to 2
- b_codes: bfloat16 [16384, 1024], P(('seq', 'tp')), may hold values from -4 to 4
- b_exps: int32 [16384, 8], P(('seq', 'tp')), may hold values from -2 to 2
- c_codes: bfloat16 [16384, 1024], P(('seq', 'tp')), may hold values from -4 to 4
- c_exps: int32 [16384, 8], P(('seq', 'tp')), may hold values from -2 to 2
- z_gate: bfloat16 [16384, 8192], P('seq', 'tp'), may hold values from -6 to 6
- dt_raw: bfloat16 [16384, 128], P('seq', 'tp'), may hold values from -4 to 4
- dt_bias: float32 [128], P('tp'), may hold values from -6 to -1.5
- a_log: float32 [128], P('tp'), may hold values from -14 to 2
- d_skip: float32 [128], P('tp'), may hold values from 0.5 to 2
- norm_gain: float32 [8192], P('tp'), may hold values from 0.5 to 1.5
- doc_starts: int32 [8], replicated, may hold values from 1 to 16383, as said below
Outputs:
- mixer_out: bfloat16 [16384, 8192], P('seq', 'tp')
Inputs may be any that keep to these rules, and one draw needn't show every extreme that they name: `doc_starts`: distinct and increasing; token 0 begins a document as well; the last entry is always 16384 - 1, a final document of one token.
All inputs are finite; a program needn't handle non-finite values.
Results may differ from a plain program's by a relative error of at most 0.0055.
Values may be sent and summed in bfloat16 or wider, within the bound.
A program may use at most 192 MiB of HBM per device.

v0:
```python
import jax
import jax.numpy as jnp
from jax import lax
from jax.sharding import PartitionSpec as P

P_SIZE = 64
N = 128
SPAN = 128


def carried_in(part, axis, combine, identity):
    place = lax.axis_index(axis)
    gathered = jax.tree.map(lambda a: lax.all_gather(a, axis), part)
    state = jax.tree.map(lambda a, e: jnp.zeros_like(a) + jnp.asarray(e, a.dtype), part, identity)

    def one(step, state):
        return combine(
            state, jax.tree.map(lambda a: lax.dynamic_index_in_dim(a, step, 0, False), gathered)
        )

    return lax.fori_loop(0, place, one, state)


def dequantize(codes, scales):
    rows, width = codes.shape
    blocks = scales.shape[1]
    grown = codes.astype(jnp.float32).reshape(rows, blocks, width // blocks)
    grown = grown * jnp.exp2(scales.astype(jnp.float32))[:, :, None]
    return grown.reshape(rows, width).astype(jnp.bfloat16)


def combine_states(earlier, later):
    return (earlier[0] * later[0], later[0][:, None, None] * earlier[1] + later[1])


def inner_mixing(cum, same, dt_blocks, x_blocks, b_blocks, c_blocks, blocks, groups, per_group):
    gap = cum[:, :, None, :] - cum[:, None, :, :]
    decay = jnp.exp(jnp.where(same[..., None], gap, -jnp.inf))
    intersection = jnp.einsum(
        "bign,bjgn->bgij", c_blocks, b_blocks, preferred_element_type=jnp.float32
    )
    mixing = (
        jnp.transpose(intersection, (0, 2, 3, 1))[..., None]
        * decay.reshape(blocks, SPAN, SPAN, groups, per_group)
        * dt_blocks.reshape(blocks, 1, SPAN, groups, per_group)
    ).astype(jnp.bfloat16)
    return jnp.einsum("bijgk,bjgkp->bigkp", mixing, x_blocks, preferred_element_type=jnp.float32)


def body(
    x_codes,
    x_exps,
    b_codes,
    b_exps,
    c_codes,
    c_exps,
    z_gate,
    dt_raw,
    dt_bias,
    a_log,
    d_skip,
    norm_gain,
    doc_starts,
):
    moved = (
        lax.all_to_all(x_codes, "tp", split_axis=1, concat_axis=0, tiled=True),
        lax.all_to_all(x_exps.astype(jnp.bfloat16), "tp", split_axis=1, concat_axis=0, tiled=True),
        lax.all_to_all(b_codes, "tp", split_axis=1, concat_axis=0, tiled=True),
        lax.all_to_all(b_exps.astype(jnp.bfloat16), "tp", split_axis=1, concat_axis=0, tiled=True),
        lax.all_to_all(c_codes, "tp", split_axis=1, concat_axis=0, tiled=True),
        lax.all_to_all(c_exps.astype(jnp.bfloat16), "tp", split_axis=1, concat_axis=0, tiled=True),
    )
    x_values = dequantize(moved[0], moved[1])
    b_values = dequantize(moved[2], moved[3])
    c_values = dequantize(moved[4], moved[5])
    rows = x_values.shape[0]
    heads = dt_raw.shape[1]
    groups = b_values.shape[1] // N
    per_group = heads // groups
    blocks = rows // SPAN
    first_row = lax.axis_index("seq") * rows
    position = first_row + jnp.arange(rows, dtype=jnp.int32)
    document = jnp.sum((doc_starts[None, :] <= position[:, None]).astype(jnp.int32), axis=1)
    before_doc = jnp.sum((doc_starts <= first_row - 1).astype(jnp.int32))
    prior = jnp.concatenate([before_doc[None], document[SPAN - 1 : -1 : SPAN]])
    step_dt = jax.nn.softplus(dt_raw.astype(jnp.float32) + dt_bias)
    rate = -step_dt * jnp.exp(a_log)
    dt_blocks = step_dt.reshape(blocks, SPAN, heads)
    cum = jnp.cumsum(rate.reshape(blocks, SPAN, heads), axis=1)
    doc_blocks = document.reshape(blocks, SPAN)
    order = jnp.arange(SPAN, dtype=jnp.int32)
    causal = order[:, None] >= order[None, :]
    same = (doc_blocks[:, :, None] == doc_blocks[:, None, :]) & causal[None]
    x_blocks = x_values.reshape(blocks, SPAN, groups, per_group, P_SIZE)
    b_blocks = b_values.reshape(blocks, SPAN, groups, N)
    c_blocks = c_values.reshape(blocks, SPAN, groups, N)
    inner = inner_mixing(
        cum, same, dt_blocks, x_blocks, b_blocks, c_blocks, blocks, groups, per_group
    )
    tail = (
        jnp.where((doc_blocks == doc_blocks[:, -1:])[..., None], jnp.exp(cum[:, -1:, :] - cum), 0.0)
        * dt_blocks
    )
    scaled = (tail.reshape(blocks, SPAN, groups, per_group)[..., None] * x_blocks).astype(
        jnp.bfloat16
    )
    block_states = jnp.einsum(
        "bjgkp,bjgn->bgkpn", scaled, b_blocks, preferred_element_type=jnp.float32
    ).reshape(blocks, heads, P_SIZE, N)
    carry_gain = jnp.exp(cum[:, -1, :]) * (doc_blocks[:, -1] == prior).astype(jnp.float32)[:, None]
    running = jnp.zeros((heads, P_SIZE, N), jnp.float32)
    gain_run = jnp.ones((heads,), jnp.float32)
    inside = []
    through = []
    for block in range(blocks):
        inside.append(running)
        through.append(gain_run)
        running = carry_gain[block][:, None, None] * running + block_states[block]
        gain_run = carry_gain[block] * gain_run
    carried = carried_in(
        (gain_run, running),
        "seq",
        combine_states,
        (jnp.ones_like(gain_run), jnp.zeros_like(running)),
    )
    entering_dev = carried[1]
    entering = jnp.stack(
        [inside[block] + through[block][:, None, None] * entering_dev for block in range(blocks)]
    ).astype(jnp.bfloat16)
    reach = jnp.where((doc_blocks == prior[:, None])[..., None], jnp.exp(cum), 0.0)
    from_state = jnp.einsum(
        "bign,bgkpn->bigkp",
        c_blocks,
        entering.reshape(blocks, groups, per_group, P_SIZE, N),
        preferred_element_type=jnp.float32,
    )
    from_state = from_state * reach.reshape(blocks, SPAN, groups, per_group)[..., None]
    skip_term = d_skip.reshape(groups, per_group)[None, None, :, :, None] * x_blocks.astype(
        jnp.float32
    )
    mixed = (inner + from_state + skip_term).reshape(rows, heads * P_SIZE)
    gated = mixed * jax.nn.silu(z_gate.astype(jnp.float32))
    grouped = gated.reshape(rows, groups, heads * P_SIZE // groups)
    power = jnp.mean(grouped * grouped, axis=2, keepdims=True)
    normed = (grouped * lax.rsqrt(power + 1e-05)).reshape(rows, heads * P_SIZE) * norm_gain
    return normed.astype(jnp.bfloat16)


def solution(mesh):
    placed = (
        P(("seq", "tp"), None),
        P(("seq", "tp"), None),
        P(("seq", "tp"), None),
        P(("seq", "tp"), None),
        P(("seq", "tp"), None),
        P(("seq", "tp"), None),
        P("seq", "tp"),
        P("seq", "tp"),
        P("tp"),
        P("tp"),
        P("tp"),
        P("tp"),
        P(),
    )
    return jax.shard_map(
        body, mesh=mesh, in_specs=placed, out_specs=P("seq", "tp"), check_vma=False
    )
```

profile of v0, /device:TPU:231, one launch (start us, length us, event | category | flops | bytes accessed | tf_op | source)
XLA Modules:
  0.0 406.7 jit_solution(2053498176050991429)
XLA Ops:
  7.9 4.2 %all-to-all-start.5 = ((bf16[64,4,2]{0,2,1:T(2,128)(2,1)}), bf16[64,4,2]{0,2,1:T(2,128)(2,1)S(1)}, u32[]{:S(2)}, u32[]{:S(2)}) async-start(bf16[64,4,2]{0,2,1:T(2,128)(2,1)} %bitcast.9), calls=%async_computation.5 | async-start | bytes 4096 | tf_op jit(solution)/shard_map/all_to_all | solution.py:69
  22.0 4.2 %all-to-all-start.1 = ((bf16[4,2,512]{2,1,0:T(2,128)(2,1)}), bf16[4,2,512]{2,1,0:T(2,128)(2,1)S(1)}, u32[]{:S(2)}, u32[]{:S(2)}) async-start(bf16[4,2,512]{2,1,0:T(2,128)(2,1)} %reshape.263), calls=%async_computation.1 | async-start | bytes 16384 | tf_op jit(solution)/shard_map/all_to_all | solution.py:67
  26.3 1.6 copy.161
  27.8 2.5 all-to-all-done.1
  30.4 3.3 all-to-all-start.4
  35.3 3.2 all-to-all-done.4
  38.5 3.5 all-to-all-start
  42.7 10.3 %all-to-all-done = bf16[64,4,2048]{2,0,1:T(8,128)(2,1)S(1)} async-done(((bf16[64,4,2048]{2,0,1:T(8,128)(2,1)}), bf16[64,4,2048]{2,0,1:T(8,128)(2,1)S(1)}, u32[]{:S(2)}, u32[]{:S(2)}) %all-to-all-start) | async-done | bytes 1048608 | tf_op jit(solution)/shard_map/all_to_all | solution.py:66
  53.2 3.0 reshape.246
  56.3 3.8 copy.113
  63.4 3.2 all-to-all-start.3
  66.8 41.2 %all-gather = f32[64,1,32]{2,1,0:T(1,128)S(1)} all-gather(f32[1,1,32]{2,1,0:T(1,128)S(1)} %get-tuple-element.74), channel_id=1, replica_groups=mesh['seq'=64,'tp'=4] {'seq'}, dimensions={0}, use_global_device_ids=true | all-gather | bytes 8320 | tf_op jit(solution)/shard_map/all_gather | solution.py:13
  107.9 1.6 copy.162
  111.6 4.5 %all-to-all-start.2 = ((bf16[64,4,256]{2,0,1:T(8,128)(2,1)}), bf16[64,4,256]{2,0,1:T(8,128)(2,1)S(1)}, u32[]{:S(2)}, u32[]{:S(2)}) async-start(bf16[64,4,256]{2,0,1:T(8,128)(2,1)} %bitcast.110), calls=%async_computation.2 | async-start | bytes 262144 | tf_op jit(solution)/shard_map/all_to_all | solution.py:70
  116.1 4.7 %all-to-all-done.2 = bf16[64,4,256]{2,0,1:T(8,128)(2,1)S(1)} async-done(((bf16[64,4,256]{2,0,1:T(8,128)(2,1)}), bf16[64,4,256]{2,0,1:T(8,128)(2,1)S(1)}, u32[]{:S(2)}, u32[]{:S(2)}) %all-to-all-start.2) | async-done | bytes 131104 | tf_op jit(solution)/shard_map/all_to_all | solution.py:70
  121.4 4.1 %fusion = f32[2,2,16,64,128]{4,3,2,1,0:T(8,128)} fusion(bf16[2,128,2,16,64]{1,4,3,2,0:T(8,128)(2,1)S(1)} %multiply_convert_fusion.2, f32[2,128,2,16]{1,3,2,0:T(8,128)} %get-tuple-element.68, f32[2,128,2,16]{1,3,2,0:T(8,128)S(1)} %bitcast.126, f32[2,128,128,2]{2,1,3,0:T(8,128)S(1)} %convolution_bitcast_fusion, pred[2,128,128]{2,1,0:T(8,128)(4,1)S(1)} %compare_and_fusion), kind=kOutput, calls=%fused_computation.7 | convolution fusion | flops 139460608 | bytes 3506176 | tf_op jit(solution)/shard_map/bijgk,bjgkp->bigkp/dot_general | solution.py:47
  125.5 173.1 %all-gather.3.cloned.1.call-done = f32[64,32,64,128]{3,2,1,0:T(8,128)} async-done(((f32[1,32,64,128]{3,2,1,0:T(8,128)}), f32[64,32,64,128]{3,2,1,0:T(8,128)}) %all-gather.3.cloned.1.call-update) | async-done | bytes 67108880 | tf_op jit(solution)/shard_map/all_gather | solution.py:13
  298.7 94.3 %while.12 = (s32[]{:T(128)}, f32[32,64,128]{2,1,0:T(8,128)S(1)}, s32[]{:T(128)}, f32[64,32]{1,0:T(8,128)S(1)}, f32[64,32,64,128]{3,2,1,0:T(8,128)}, /*index=5*/s32[]{:T(128)}, s32[]{:T(128)}, s32[]{:T(128)}) while((s32[]{:T(128)}, f32[32,64,128]{2,1,0:T(8,128)S(1)}, s32[]{:T(128)}, f32[64,32]{1,0:T(8,128)S(1)}, f32[64,32,64,128]{3,2,1,0:T(8,128)}, ...), condition=%wide.region_4.5_spmd, body=%wide.region_3.4_spmd.sunk | while | flops 524293 | bytes 3146239 | solution.py:21
  298.8 1.4 bitcast_add_fusion.3
  300.3 1.4 bitcast_add_fusion.3
  301.7 1.4 bitcast_add_fusion.3
  303.2 1.4 bitcast_add_fusion.3
  304.7 1.4 bitcast_add_fusion.3
  306.2 1.4 bitcast_add_fusion.3
  307.7 1.4 bitcast_add_fusion.3
  309.2 1.4 bitcast_add_fusion.3
  310.7 1.4 bitcast_add_fusion.3
  312.2 1.4 bitcast_add_fusion.3
  313.7 1.4 bitcast_add_fusion.3
  315.2 1.4 bitcast_add_fusion.3
  316.7 1.4 bitcast_add_fusion.3
  318.2 1.4 bitcast_add_fusion.3
  319.7 1.4 bitcast_add_fusion.3
  321.2 1.4 bitcast_add_fusion.3
  322.7 1.4 bitcast_add_fusion.3
  324.2 1.4 bitcast_add_fusion.3
  325.7 1.4 bitcast_add_fusion.3
  327.2 1.4 bitcast_add_fusion.3
  328.7 1.4 bitcast_add_fusion.3
  330.2 1.4 bitcast_add_fusion.3
  331.7 1.4 bitcast_add_fusion.3
  333.2 1.4 bitcast_add_fusion.3
  334.7 1.4 bitcast_add_fusion.3
  336.2 1.4 bitcast_add_fusion.3
  337.7 1.4 bitcast_add_fusion.3
  339.2 1.4 bitcast_add_fusion.3
  340.7 1.4 bitcast_add_fusion.3
  342.1 1.4 bitcast_add_fusion.3
  343.6 1.4 bitcast_add_fusion.3
  345.1 1.4 bitcast_add_fusion.3
  346.6 1.4 bitcast_add_fusion.3
  348.1 1.4 bitcast_add_fusion.3
  349.6 1.4 bitcast_add_fusion.3
  351.1 1.4 bitcast_add_fusion.3
  352.6 1.4 bitcast_add_fusion.3
  354.1 1.4 bitcast_add_fusion.3
  355.6 1.4 bitcast_add_fusion.3
  357.1 1.4 bitcast_add_fusion.3
  358.6 1.4 bitcast_add_fusion.3
  360.1 1.4 bitcast_add_fusion.3
  361.6 1.4 bitcast_add_fusion.3
  369.1 1.4 bitcast_add_fusion.3
  390.0 1.4 bitcast_add_fusion.3
  395.2 1.7 copy.126
  (171 shorter events, 51.6 us)
Async XLA Ops:
  6.5 27.8 %copy-start.4 = (bf16[64,8192]{1,0:T(8,128)(2,1)S(1)}, bf16[64,8192]{1,0:T(8,128)(2,1)}, u32[]{:S(2)}) copy-start(bf16[64,8192]{1,0:T(8,128)(2,1)} %param.15) | copy-start | bytes 3145732
  7.9 14.1 %all-to-all-start.5 = ((bf16[64,4,2]{0,2,1:T(2,128)(2,1)}), bf16[64,4,2]{0,2,1:T(2,128)(2,1)S(1)}, u32[]{:S(2)}, u32[]{:S(2)}) async-start(bf16[64,4,2]{0,2,1:T(2,128)(2,1)} %bitcast.9), calls=%async_computation.5 | async-start | bytes 4096 | tf_op jit(solution)/shard_map/all_to_all | solution.py:69
  22.0 8.4 %all-to-all-start.1 = ((bf16[4,2,512]{2,1,0:T(2,128)(2,1)}), bf16[4,2,512]{2,1,0:T(2,128)(2,1)S(1)}, u32[]{:S(2)}, u32[]{:S(2)}) async-start(bf16[4,2,512]{2,1,0:T(2,128)(2,1)} %reshape.263), calls=%async_computation.1 | async-start | bytes 16384 | tf_op jit(solution)/shard_map/all_to_all | solution.py:67
  30.4 8.1 %all-to-all-start.4 = ((bf16[64,4,256]{2,0,1:T(8,128)(2,1)}), bf16[64,4,256]{2,0,1:T(8,128)(2,1)S(1)}, u32[]{:S(2)}, u32[]{:S(2)}) async-start(bf16[64,4,256]{2,0,1:T(8,128)(2,1)} %bitcast.109), calls=%async_computation.4 | async-start | bytes 262144 | tf_op jit(solution)/shard_map/all_to_all | solution.py:68
  38.5 14.5 %all-to-all-start = ((bf16[64,4,2048]{2,0,1:T(8,128)(2,1)}), bf16[64,4,2048]{2,0,1:T(8,128)(2,1)S(1)}, u32[]{:S(2)}, u32[]{:S(2)}) async-start(bf16[64,4,2048]{2,0,1:T(8,128)(2,1)} %bitcast.108), calls=%async_computation | async-start | bytes 2097152 | tf_op jit(solution)/shard_map/all_to_all | solution.py:66
  42.0 256.6 %all-gather.3.cloned.1.call-start = ((), (), s32[]{:S(2)}) async-start(), calls=%async_computation.6 | async-start | bytes 68157440 | tf_op jit(solution)/shard_map/all_gather | solution.py:13
  42.1 19.1 %copy-start.8 = (f32[32]{0:T(128)}, f32[32]{0:T(128)S(1)}, u32[]{:S(2)}) copy-start(f32[32]{0:T(128)S(1)} %broadcast_multiply_fusion.1) | copy-start | bytes 388
  42.7 17.7 %copy-start.1 = (f32[2,128,2,128]{3,2,1,0:T(2,128)}, f32[2,128,2,128]{3,2,1,0:T(2,128)S(1)}, u32[]{:S(2)}) copy-start(f32[2,128,2,128]{3,2,1,0:T(2,128)S(1)} %reshape.248) | copy-start | bytes 786436
  60.9 0.6 copy-start.11
  61.5 1.3 copy-start.7
  61.5 48.7 %copy-start.5 = (bf16[256,2048]{1,0:T(8,128)(2,1)S(1)}, bf16[256,2048]{1,0:T(8,128)(2,1)}, u32[]{:S(2)}) copy-start(bf16[256,2048]{1,0:T(8,128)(2,1)} %param.21) | copy-start | bytes 3145732
  62.8 58.2 %copy-start.2 = (f32[2,128,2,128]{3,2,1,0:T(2,128)S(1)}, f32[2,128,2,128]{3,2,1,0:T(2,128)}, u32[]{:S(2)}) copy-start(f32[2,128,2,128]{3,2,1,0:T(2,128)} %copy-done.1) | copy-start | bytes 786436
  63.4 48.2 %all-to-all-start.3 = ((bf16[64,4,2]{0,2,1:T(2,128)(2,1)}), bf16[64,4,2]{0,2,1:T(2,128)(2,1)S(1)}, u32[]{:S(2)}, u32[]{:S(2)}) async-start(bf16[64,4,2]{0,2,1:T(2,128)(2,1)} %bitcast.6), calls=%async_computation.3 | async-start | bytes 4096 | tf_op jit(solution)/shard_map/all_to_all | solution.py:71
  111.6 9.3 %all-to-all-start.2 = ((bf16[64,4,256]{2,0,1:T(8,128)(2,1)}), bf16[64,4,256]{2,0,1:T(8,128)(2,1)S(1)}, u32[]{:S(2)}, u32[]{:S(2)}) async-start(bf16[64,4,256]{2,0,1:T(8,128)(2,1)} %bitcast.110), calls=%async_computation.2 | async-start | bytes 262144 | tf_op jit(solution)/shard_map/all_to_all | solution.py:70
  298.7 94.3 %copy-start.9 = (f32[32]{0:T(128)S(1)}, f32[32]{0:T(128)}, u32[]{:S(2)}) copy-start(f32[32]{0:T(128)} %copy-done.8) | copy-start | bytes 388
  298.7 94.3 %copy-start.10 = (f32[32]{0:T(128)S(1)}, f32[32]{0:T(128)}, u32[]{:S(2)}) copy-start(f32[32]{0:T(128)} %get-tuple-element.73) | copy-start | bytes 388
  393.0 1.6 copy-start.3
  395.2 1.7 copy-start
  396.9 0.7 copy-start.6
Sparse Core Ops, SparseCore 0:
  62.9 235.6 all-gather.2
where the time goes:
time: 410 us; the launch traced here: 407 us
  waiting for transfers between devices  194 us (47%)
  other arithmetic  104 us (25%)
  blocking collectives  41.2 us (10%)
  starting transfers between devices  23 us (6%)
  local copies, waits for them, and re-layouts  22.7 us (6%)
  between operations  13.8 us (3%)
  matrix products  5.6 us (1%)
    all_gather x1, waiting for transfers between devices, carried_in(): gathered = jax.tree.map(lambda a: lax.all_gather(a, axis), part)  173 us
    add x63, other arithmetic, combine_states(): later[0][:, None, None] * earlier[1] + later[1]  91.2 us
    all_gather x1, blocking collectives, carried_in(): gathered = jax.tree.map(lambda a: lax.all_gather(a, axis), part)  41.2 us
    all_to_all x1, waiting for transfers between devices, body(): lax.all_to_all(x_codes, 'tp', split_axis=1, concat_axis=0, tiled=True)  10.3 us
  transfers between devices with their start and end apart: 7, of which 5 were waited for; matrix products, arithmetic and copies ran while one was open for 6% of the time, Pallas kernels for 0%

commit v1 on v0

v1 whole, which is shorter than its diff:
```python
import functools

import jax
import jax.numpy as jnp
from jax import lax
from jax.experimental import pallas as pl
from jax.experimental.pallas import tpu as pltpu
from jax.sharding import PartitionSpec as P

F32 = jnp.float32
BF16 = jnp.bfloat16
P_SIZE = 64
N = 128
SPAN = 128
QB = 128
EPS = 1e-05
NX, NZ, NC, NT = 4, 8, 2, 4


def split3(v):
    hi = v.astype(BF16)
    rest = v - hi.astype(F32)
    mid = rest.astype(BF16)
    low = (rest - mid.astype(F32)).astype(BF16)
    return hi, mid, low


def dot(a, b):
    return jnp.dot(a, b, preferred_element_type=F32)


def kernel(
    x_hbm,
    xe_ref,
    b_ref,
    be_ref,
    c_ref,
    ce_ref,
    z_hbm,
    dtr_ref,
    bias_ref,
    alog_ref,
    skip_ref,
    gain_ref,
    starts_ref,
    out_hbm,
    xs,
    bs,
    cs,
    zbuf,
    xbuf,
    bbuf,
    cbuf,
    cumc,
    turn_in,
    turned,
    tailx,
    reachx,
    rows_in,
    rows_ex,
    gsend,
    gpair,
    gz,
    gx,
    sfirst,
    sdev,
    sdev16,
    pairs,
    tot16,
    zbuf_in,
    prefix,
    xsend,
    xin,
    esend,
    ein,
    keep,
    psend,
    ent,
    cbm,
    acc,
    obuf,
    load_sem,
    out_sem,
    own_sem,
    y_send,
    y_recv,
    g_send,
    g_recv,
    p_send,
    p_recv,
    z_send,
    z_recv,
    l_send,
    l_recv,
):
    rows = xbuf.shape[0]
    slab = rows // NT
    heads = dtr_ref.shape[1]
    width = xbuf.shape[1]
    groups = bbuf.shape[1] // N
    per_group = heads // groups
    gw = width // groups
    half = gw // NC
    zr = N // NZ
    blocks = rows // SPAN

    s = lax.axis_index("seq")
    t = lax.axis_index("tp")
    xx = s // (NZ * NC)
    zz = (s // NC) % NZ
    cc = s % NC
    mate = s + 1 - 2 * cc

    def y_dev(k):
        return {"seq": s, "tp": (t + k) % NT}

    def z_dev(k):
        return {"seq": xx * (NZ * NC) + ((zz + k) % NZ) * NC + cc, "tp": t}

    def x_dev(k):
        return {"seq": ((xx + k) % NX) * (NZ * NC) + zz * NC + cc, "tp": t}

    mate_dev = {"seq": mate, "tp": t}

    barrier = pltpu.get_barrier_semaphore()

    def greet(dev):
        pl.semaphore_signal(barrier, inc=1, device_id=dev, device_id_type=pl.DeviceIdType.MESH)

    x_load = pltpu.make_async_copy(x_hbm, xs, load_sem.at[0])
    x_load.start()
    z_load = pltpu.make_async_copy(z_hbm, zbuf, load_sem.at[1])
    z_load.start()

    def greet_loop(make):
        def one(k, _):
            greet(make(k))
            return 0

        return one

    lax.fori_loop(1, NT, greet_loop(y_dev), 0)
    lax.fori_loop(1, NZ, greet_loop(z_dev), 0)
    lax.fori_loop(1, NX, greet_loop(x_dev), 0)
    greet(mate_dev)

    def remote(src, dst, send, recv, dev):
        return pltpu.make_async_remote_copy(
            src_ref=src,
            dst_ref=dst,
            send_sem=send,
            recv_sem=recv,
            device_id=dev,
            device_id_type=pl.DeviceIdType.MESH,
        )

    def y_copy(piece, k):
        to = (t + k) % NT
        mine = pl.ds(pl.multiple_of(t * slab, slab), slab)
        if piece == 0 or piece == groups + 1:
            src, dst = (bs, bbuf) if piece == 0 else (cs, cbuf)
            w = groups * N
            src = src.at[:, pl.ds(pl.multiple_of(to * w, w), w)]
            dst = dst.at[mine, :]
        else:
            g = piece - 1
            src = xs.at[:, pl.ds(pl.multiple_of(to * width + g * gw, gw), gw)]
            dst = xbuf.at[mine, pl.ds(g * gw, gw)]
        return remote(src, dst, y_send.at[piece, k], y_recv.at[piece, k], y_dev(k))

    def y_own(piece):
        mine = pl.ds(pl.multiple_of(t * slab, slab), slab)
        if piece == 0 or piece == groups + 1:
            src, dst = (bs, bbuf) if piece == 0 else (cs, cbuf)
            w = groups * N
            src = src.at[:, pl.ds(pl.multiple_of(t * w, w), w)]
            dst = dst.at[mine, :]
        else:
            g = piece - 1
            src = xs.at[:, pl.ds(pl.multiple_of(t * width + g * gw, gw), gw)]
            dst = xbuf.at[mine, pl.ds(g * gw, gw)]
        return pltpu.make_async_copy(src, dst, own_sem.at[piece])

    def y_start(piece):
        def one(k, _):
            y_copy(piece, k).start()
            return 0

        lax.fori_loop(1, NT, one, 0)
        y_own(piece).start()

    def y_wait(piece):
        def one(k, _):
            y_copy(piece, k).wait_recv()
            return 0

        lax.fori_loop(1, NT, one, 0)
        y_own(piece).wait()

    def scale_cols(src, dst, exps, cols):
        for j in cols:
            at = slice(j * QB, (j + 1) * QB)
            dst[:, at] = (src[:, at].astype(F32) * exps[:, j : j + 1]).astype(BF16)

    per_x = gw // QB
    xe = jnp.exp2(xe_ref[...].astype(F32))
    be = jnp.exp2(be_ref[...].astype(F32))
    ce = jnp.exp2(ce_ref[...].astype(F32))

    def x_cols(g):
        return [d * groups * per_x + g * per_x + j for d in range(NT) for j in range(per_x)]

    scale_cols(b_ref, bs, be, range(NT * groups))
    x_load.wait()
    scale_cols(xs, xs, xe, x_cols(0))
    pl.semaphore_wait(barrier, (NT - 1) + (NZ - 1) + (NX - 1) + 1)
    y_start(0)
    y_start(1)
    for g in range(1, groups):
        scale_cols(xs, xs, xe, x_cols(g))
        y_start(1 + g)
    scale_cols(c_ref, cs, ce, range(NT * groups))
    y_start(groups + 1)

    def document(position):
        total = jnp.zeros(position.shape, jnp.int32)
        for k in range(starts_ref.shape[0]):
            total = total + (starts_ref[k] <= position).astype(jnp.int32)
        return total

    first = s * rows
    row_i = lax.broadcasted_iota(jnp.int32, (SPAN, SPAN), 0)
    col_i = lax.broadcasted_iota(jnp.int32, (SPAN, SPAN), 1)
    one_row = jnp.zeros((1, SPAN), jnp.int32)

    raw = dtr_ref[...].astype(F32) + bias_ref[...]
    step = jnp.maximum(raw, 0.0) + jnp.log1p(jnp.exp(-jnp.abs(raw)))
    rate = -step * jnp.exp(alog_ref[...])
    tri = (row_i >= col_i).astype(BF16)
    turn_in[...] = jnp.zeros_like(turn_in)
    lead = lax.broadcasted_iota(jnp.int32, (heads, width), 0)
    chan = lax.broadcasted_iota(jnp.int32, (heads, width), 1)
    spread = (lead == chan // P_SIZE).astype(BF16)

    def grow(v, parts):
        pieces = split3(v)[:parts]
        total = dot(pieces[0], spread)
        for piece in pieces[1:]:
            total = total + dot(piece, spread)
        return total

    same = []
    gains = []
    for b in range(blocks):
        at = slice(b * SPAN, (b + 1) * SPAN)
        parts = split3(rate[at])
        cum = dot(tri, parts[0]) + dot(tri, parts[1]) + dot(tri, parts[2])
        base = first + b * SPAN
        doc_i = document(base + row_i)
        doc_j = document(base + col_i)
        same.append((doc_i == doc_j) & (row_i >= col_i))
        doc_last = document(base + SPAN - 1 + one_row)
        prior = document(base - 1 + one_row)
        last = cum[SPAN - 1 : SPAN, :]
        cumc[at, :] = cum
        turn_in[b, :, :heads] = cum
        turn_in[b, :, heads : 2 * heads] = step[at]
        tail = jnp.where(
            doc_i[:, :heads] == doc_last[:, :heads], jnp.exp(jnp.minimum(last - cum, 0.0)), 0.0
        )
        tailx[at, :] = grow(tail * step[at], 2)
        reach = jnp.where(doc_i[:, :heads] == prior[:, :heads], jnp.exp(cum), 0.0)
        reachx[at, :] = grow(reach, 2)
        gains.append(jnp.where(doc_last[:, :heads] == prior[:, :heads], jnp.exp(last), 0.0))
        turned[b] = jnp.transpose(turn_in[b])

    gdev = gains[0]
    for b in range(1, blocks):
        gdev = gdev * gains[b]

    gsend[...] = jnp.zeros_like(gsend)
    gsend[0, 0:1, :heads] = gdev
    pair_g = remote(gsend.at[0], gpair, g_send.at[0], g_recv.at[0], mate_dev)
    pair_g.start()

    def z_gain(k):
        return remote(gsend.at[1], gz.at[zz], g_send.at[k], g_recv.at[k], z_dev(k))

    def x_gain(k):
        return remote(
            gsend.at[2], gx.at[xx], g_send.at[NZ - 1 + k], g_recv.at[NZ - 1 + k], x_dev(k)
        )

    def loop(n, make, what):
        def one(k, _):
            getattr(make(k), what)()
            return 0

        lax.fori_loop(1, n, one, 0)

    pair_g.wait_recv()
    gother = gpair[0:1, :heads]
    gfirst = jnp.where(cc == 0, gdev, gother)
    gsecond = jnp.where(cc == 0, gother, gdev)
    gsend[1, 0:1, :heads] = gfirst * gsecond
    gz[pl.ds(zz, 1)] = gsend[1:2]
    loop(NZ, z_gain, "start")

    z_load.wait()

    loop(NZ, z_gain, "wait_recv")
    gline = gz[0][0:1, :heads]
    before = [jnp.ones((1, heads), F32)]
    for k in range(1, NZ):
        before.append(gline)
        gline = gline * gz[k][0:1, :heads]
    gsend[2, 0:1, :heads] = gline
    gx[pl.ds(xx, 1)] = gsend[2:3]
    loop(NX, x_gain, "start")
    rows_in[...] = jnp.zeros_like(rows_in)
    for b in range(blocks):
        rows_in[b : b + 1, :] = gains[b]
    rows_in[2:3, :] = gfirst
    rows_in[3:4, :] = gsecond
    for k in range(NZ):
        rows_in[8 + k : 9 + k, :] = gz[k][0:1, :heads]
        rows_in[16 + k : 17 + k, :] = before[k]
    loop(NX, x_gain, "wait_recv")
    for k in range(NX):
        rows_in[24 + k : 25 + k, :] = gx[k][0:1, :heads]
    rows_ex[...] = grow(rows_in[...], 3)

    def my_half(g):
        return pl.ds(pl.multiple_of(g * gw + cc * half, half), half)

    def other_half(g):
        return pl.ds(pl.multiple_of(g * gw + (1 - cc) * half, half), half)

    def pair_copy(g):
        return remote(
            sdev16.at[:, other_half(g)], pairs.at[g], p_send.at[0, g], p_recv.at[0, g], mate_dev
        )

    def states(g):
        at = slice(g * gw, (g + 1) * gw)
        state = None
        for b in range(blocks):
            ta = slice(b * SPAN, (b + 1) * SPAN)
            scaled = (tailx[ta, at] * xbuf[ta, at].astype(F32)).astype(BF16)
            bv = bbuf[ta, g * N : (g + 1) * N]
            block = lax.dot_general(
                bv, scaled, (((0,), (0,)), ((), ())), preferred_element_type=F32
            )
            if b == 0:
                sfirst[:, at] = block
                state = block
            else:
                state = rows_ex[b : b + 1, at] * state + block
        sdev[:, at] = state
        sdev16[:, at] = state.astype(BF16)
        pair_copy(g).start()

    def z_copy(g, k):
        to = (zz + k) % NZ
        return remote(
            tot16.at[g, pl.ds(pl.multiple_of(to * zr, zr), zr), :],
            zbuf_in.at[g, zz],
            z_send.at[0, g, k],
            z_recv.at[0, g, k],
            z_dev(k),
        )

    def chip_total(g):
        pair_copy(g).wait_recv()
        mine = sdev[:, my_half(g)]
        other = pairs[g].astype(F32)
        early = jnp.where(cc == 0, mine, other)
        late = jnp.where(cc == 0, other, mine)
        pairs_total = rows_ex[3:4, my_half(g)] * early + late
        keep[g] = early
        tot16[g] = pairs_total.astype(BF16)
        zbuf_in[g, pl.ds(zz, 1)] = tot16[g, pl.ds(pl.multiple_of(zz * zr, zr), zr), :][None]
        loop(NZ, functools.partial(z_copy, g), "start")

    def x_copy(g, k):
        return remote(
            xsend.at[g], xin.at[g, xx], l_send.at[g, k], l_recv.at[g, k], x_dev(k)
        )

    def line_scan(g):
        loop(NZ, functools.partial(z_copy, g), "wait_recv")
        run = jnp.zeros((zr, half), F32)
        for k in range(NZ):
            prefix[g, k] = run
            run = rows_ex[8 + k : 9 + k, my_half(g)] * run + zbuf_in[g, k].astype(F32)
        xsend[g] = run
        xin[g, pl.ds(xx, 1)] = run[None]
        loop(NX, functools.partial(x_copy, g), "start")

    def e_copy(g, k):
        to = (zz + k) % NZ
        return remote(
            esend.at[g, to],
            ein.at[g, pl.ds(pl.multiple_of(zz * zr, zr), zr), :],
            z_send.at[1, g, k],
            z_recv.at[1, g, k],
            z_dev(k),
        )

    def enter(g):
        loop(NX, functools.partial(x_copy, g), "wait_recv")
        run = jnp.zeros((zr, half), F32)
        for k in range(NX):
            after = rows_ex[24 + k : 25 + k, my_half(g)] * run + xin[g, k]
            run = jnp.where(k < xx, after, run)
        for k in range(NZ):
            esend[g, k] = (prefix[g, k] + rows_ex[16 + k : 17 + k, my_half(g)] * run).astype(BF16)
        ein[g, pl.ds(pl.multiple_of(zz * zr, zr), zr), :] = esend[g, pl.ds(zz, 1)][0]
        loop(NZ, functools.partial(e_copy, g), "start")

    def back_copy(g):
        return remote(
            psend.at[g], ent.at[:, my_half(g)], p_send.at[1, g], p_recv.at[1, g], mate_dev
        )

    def back(g):
        loop(NZ, functools.partial(e_copy, g), "wait_recv")
        at_first = ein[g].astype(F32)
        at_second = rows_ex[2:3, my_half(g)] * at_first + keep[g]
        psend[g] = jnp.where(cc == 0, at_second, at_first).astype(BF16)
        back_copy(g).start()
        ent[:, my_half(g)] = jnp.where(cc == 0, at_first, at_second).astype(BF16)

    def inner(g):
        lane = lax.broadcasted_iota(jnp.int32, (SPAN, 2 * P_SIZE), 1)

        def one(b, _):
            ta = pl.ds(pl.multiple_of(b * SPAN, SPAN), SPAN)
            cb = cbm[b, g]
            cums = cumc[ta, :]
            rows_t = turned[b]
            for pair in range(per_group // 2):
                cols = slice(g * gw + pair * 2 * P_SIZE, g * gw + (pair + 1) * 2 * P_SIZE)
                xp = xbuf[ta, cols]
                mixes = []
                for h in (g * per_group + 2 * pair, g * per_group + 2 * pair + 1):
                    gap = cums[:, h : h + 1] - rows_t[h : h + 1, :]
                    mix = cb * jnp.exp(jnp.minimum(gap, 0.0)) * rows_t[heads + h : heads + h + 1, :]
                    mixes.append(mix.astype(BF16))
                left = jnp.where(lane < P_SIZE, xp, jnp.zeros_like(xp))
                right = jnp.where(lane < P_SIZE, jnp.zeros_like(xp), xp)
                y = dot(jnp.concatenate(mixes, axis=1), jnp.concatenate([left, right], axis=0))
                acc[ta, cols] = y + skip_row[:, cols] * xp.astype(F32)
            return 0

        lax.fori_loop(0, blocks, one, 0)

    skip_row = skip_ref[...]

    def out_copy(g):
        at = pl.ds(g * gw, gw)
        return pltpu.make_async_copy(obuf.at[:, at], out_hbm.at[:, at], out_sem.at[g])

    def finish(g):
        back_copy(g).wait_recv()
        at = slice(g * gw, (g + 1) * gw)
        entering = ent[:, at]
        for b in range(blocks):
            ta = slice(b * SPAN, (b + 1) * SPAN)
            if b > 0:
                entering = (
                    rows_ex[b - 1 : b, at] * entering.astype(F32) + sfirst[:, at]
                ).astype(BF16)
            cv = cbuf[ta, g * N : (g + 1) * N]
            y = acc[ta, at] + dot(cv, entering) * reachx[ta, at]
            zf = zbuf[ta, at].astype(F32)
            gated = y * (zf / (1.0 + jnp.exp(-zf)))
            power = jnp.mean(gated * gated, axis=1, keepdims=True)
            obuf[ta, at] = (gated * lax.rsqrt(power + EPS) * gain_ref[:, at]).astype(BF16)
        out_copy(g).start()

    y_wait(0)
    y_wait(1)
    states(0)
    chip_total(0)
    line_scan(0)
    y_wait(2)
    states(1)
    enter(0)
    chip_total(1)
    y_wait(groups + 1)
    for b in range(blocks):
        ta = slice(b * SPAN, (b + 1) * SPAN)
        for g in range(groups):
            at = slice(g * N, (g + 1) * N)
            cb = lax.dot_general(
                cbuf[ta, at], bbuf[ta, at], (((1,), (1,)), ((), ())), preferred_element_type=F32
            )
            cbm[b, g] = jnp.where(same[b], cb, 0.0)
    back(0)
    line_scan(1)
    inner(0)
    enter(1)
    inner(1)
    finish(0)
    back(1)
    finish(1)

    for piece in range(groups + 2):
        loop(NT, functools.partial(y_copy, piece), "wait_send")
    pair_g.wait_send()
    loop(NZ, z_gain, "wait_send")
    loop(NX, x_gain, "wait_send")
    for g in range(groups):
        pair_copy(g).wait_send()
        loop(NZ, functools.partial(z_copy, g), "wait_send")
        loop(NX, functools.partial(x_copy, g), "wait_send")
        loop(NZ, functools.partial(e_copy, g), "wait_send")
        back_copy(g).wait_send()
        out_copy(g).wait()


def body(
    x_codes,
    x_exps,
    b_codes,
    b_exps,
    c_codes,
    c_exps,
    z_gate,
    dt_raw,
    dt_bias,
    a_log,
    d_skip,
    norm_gain,
    doc_starts,
):
    rows, width = z_gate.shape
    slab = x_codes.shape[0]
    heads = dt_raw.shape[1]
    gn = b_codes.shape[1] // NT
    groups = gn // N
    gw = width // groups
    half = gw // NC
    zr = N // NZ
    blocks = rows // SPAN
    vmem = pl.BlockSpec(memory_space=pltpu.VMEM)
    hbm = pl.BlockSpec(memory_space=pl.ANY)
    smem = pl.BlockSpec(memory_space=pltpu.SMEM)
    dma = pltpu.SemaphoreType.DMA
    return pl.pallas_call(
        kernel,
        out_shape=jax.ShapeDtypeStruct((rows, width), BF16),
        in_specs=[hbm, vmem, vmem, vmem, vmem, vmem, hbm, vmem, vmem, vmem, vmem, vmem, smem],
        out_specs=hbm,
        scratch_shapes=[
            pltpu.VMEM(x_codes.shape, BF16),
            pltpu.VMEM(b_codes.shape, BF16),
            pltpu.VMEM(c_codes.shape, BF16),
            pltpu.VMEM((rows, width), BF16),
            pltpu.VMEM((rows, width), BF16),
            pltpu.VMEM((rows, gn), BF16),
            pltpu.VMEM((rows, gn), BF16),
            pltpu.VMEM((rows, heads), F32),
            pltpu.VMEM((blocks, SPAN, SPAN), F32),
            pltpu.VMEM((blocks, SPAN, SPAN), F32),
            pltpu.VMEM((rows, width), F32),
            pltpu.VMEM((rows, width), F32),
            pltpu.VMEM((32, heads), F32),
            pltpu.VMEM((32, width), F32),
            pltpu.VMEM((3, 8, 128), F32),
            pltpu.VMEM((8, 128), F32),
            pltpu.VMEM((NZ, 8, 128), F32),
            pltpu.VMEM((NX, 8, 128), F32),
            pltpu.VMEM((N, width), F32),
            pltpu.VMEM((N, width), F32),
            pltpu.VMEM((N, width), BF16),
            pltpu.VMEM((groups, N, half), BF16),
            pltpu.VMEM((groups, N, half), BF16),
            pltpu.VMEM((groups, NZ, zr, half), BF16),
            pltpu.VMEM((groups, NZ, zr, half), F32),
            pltpu.VMEM((groups, zr, half), F32),
            pltpu.VMEM((groups, NX, zr, half), F32),
            pltpu.VMEM((groups, NZ, zr, half), BF16),
            pltpu.VMEM((groups, N, half), BF16),
            pltpu.VMEM((groups, N, half), F32),
            pltpu.VMEM((groups, N, half), BF16),
            pltpu.VMEM((N, width), BF16),
            pltpu.VMEM((blocks, groups, SPAN, SPAN), F32),
            pltpu.VMEM((rows, width), F32),
            pltpu.VMEM((rows, width), BF16),
            dma((2,)),
            dma((groups,)),
            dma((groups + 2,)),
            dma((groups + 2, NT)),
            dma((groups + 2, NT)),
            dma((NZ + NX,)),
            dma((NZ + NX,)),
            dma((2, groups)),
            dma((2, groups)),
            dma((2, groups, NZ)),
            dma((2, groups, NZ)),
            dma((groups, NX)),
            dma((groups, NX)),
        ],
        compiler_params=pltpu.CompilerParams(
            collective_id=0, has_side_effects=True, vmem_limit_bytes=48 * 1024 * 1024
        ),
    )(
        x_codes,
        x_exps,
        b_codes,
        b_exps,
        c_codes,
        c_exps,
        z_gate,
        dt_raw,
        dt_bias[None, :],
        a_log[None, :],
        jnp.repeat(d_skip, P_SIZE)[None, :],
        norm_gain[None, :],
        doc_starts,
    )


def solution(mesh):
    placed = (
        P(("seq", "tp"), None),
        P(("seq", "tp"), None),
        P(("seq", "tp"), None),
        P(("seq", "tp"), None),
        P(("seq", "tp"), None),
        P(("seq", "tp"), None),
        P("seq", "tp"),
        P("seq", "tp"),
        P("tp"),
        P("tp"),
        P("tp"),
        P("tp"),
        P(),
    )
    return jax.shard_map(
        body, mesh=mesh, in_specs=placed, out_specs=P("seq", "tp"), check_vma=False
    )
```

time: 410 us -> 62.8 us (0.15)
  the two profiles are of different devices: /device:TPU:231 before, /device:TPU:1 now
where the time goes in v1:
time: 62.8 us; the launch traced here: 62.5 us
  Pallas kernels  54.8 us (87%)
  local copies, waits for them, and re-layouts  7.6 us (12%)
    pallas_call x1, Pallas kernels, body(): pl.pallas_call(kernel, out_shape=jax.ShapeDtypeStruct((rows, width), BF16...  54.8 us
    unnamed x22, local copies, waits for them, and re-layouts  6.76 us

profile of v1, /device:TPU:1, one launch (start us, length us, event | category | flops | bytes accessed | tf_op | source)
XLA Modules:
  0.0 62.5 jit_solution(7248046125914797972)
XLA Ops:
  0.0 0.0 copy-start.2
  0.0 0.8 %broadcast_in_dim.14 = f32[32,64]{1,0:T(8,128)S(1)} broadcast(f32[32]{0:T(128)} %param.23), dimensions={0} | broadcast | bytes 8320 | tf_op jit(solution)/shard_map/broadcast_in_dim | solution.py:620
  0.8 0.1 broadcast_in_dim_reshape.3.skip_ref
  0.8 0.8 %copy.14.be_ref = s32[64,8]{1,0:T(8,128)S(1)} copy(s32[64,8]{0,1:T(8,128)} %param.16) | data formatting | bytes 4096 | tf_op args[3]
  1.6 0.8 %copy.15.ce_ref = s32[64,8]{1,0:T(8,128)S(1)} copy(s32[64,8]{0,1:T(8,128)} %param.18) | data formatting | bytes 4096 | tf_op args[5]
  2.4 0.0 copy-start.4
  2.4 0.0 copy-start.5
  2.4 0.0 copy-start.6
  2.4 0.0 copy-start.7
  2.4 0.0 copy-start.8
  2.4 0.9 %copy.16.dtr_ref = bf16[256,32]{1,0:T(8,128)(2,1)S(1)} copy(bf16[256,32]{0,1:T(8,128)(2,1)} %param.20) | data formatting | bytes 32768 | tf_op args[7]
  3.3 0.0 copy-done.2
  3.3 0.0 copy-done.4
  3.3 0.0 copy-done.5
  3.3 0.0 copy-done.6
  3.3 0.0 copy-done.7
  3.3 0.0 copy-done.8
  3.4 0.0 copy-start
  3.4 1.2 %copy-done = bf16[64,8192]{1,0:T(8,128)(2,1)S(1)} copy-done((bf16[64,8192]{1,0:T(8,128)(2,1)S(1)}, bf16[64,8192]{1,0:T(8,128)(2,1)}, u32[]{:S(2)}) %copy-start) | copy-done | bytes 1048600
  4.6 0.0 copy-start.1
  4.6 1.2 %copy-done.1 = bf16[256,2048]{1,0:T(8,128)(2,1)S(1)} copy-done((bf16[256,2048]{1,0:T(8,128)(2,1)S(1)}, bf16[256,2048]{1,0:T(8,128)(2,1)}, u32[]{:S(2)}) %copy-start.1) | copy-done | bytes 1048600
  5.8 0.0 copy-start.3
  5.8 0.9 %copy-done.3 = bf16[64,1024]{1,0:T(8,128)(2,1)S(1)} copy-done((bf16[64,1024]{1,0:T(8,128)(2,1)S(1)}, bf16[64,1024]{1,0:T(8,128)(2,1)}, u32[]{:S(2)}) %copy-start.3) | copy-done | bytes 131096
  6.7 54.8 %shard_map.127 = bf16[256,2048]{1,0:T(8,128)(2,1)S(1)} custom-call(bf16[64,8192]{1,0:T(8,128)(2,1)S(1)} %copy-done, s32[64,64]{1,0:T(8,128)S(1)} %copy-done.4, bf16[64,1024]{1,0:T(8,128)(2,1)S(1)} %copy-done.2, s32[64,8]{1,0:T(8,128)S(1)} %copy.14.be_ref, bf16[64,1024]{1,0:T(8,128)(2,1)S(1)} %copy-done.3, s32[64,8]{1,0:T(8,128)S(1)} %copy.15.ce_ref, ...), custom_call_target="tpu_custom_call" | custom-call | tf_op jit(solution)/shard_map/pallas_call | solution.py:551
  61.5 1.0 %copy.18 = bf16[256,2048]{1,0:T(8,128)(2,1)} copy(bf16[256,2048]{1,0:T(8,128)(2,1)S(1)} %shard_map.127) | data formatting | bytes 2097152
Async XLA Ops:
  0.0 3.3 %copy-start.2 = (bf16[64,1024]{1,0:T(8,128)(2,1)S(1)}, bf16[64,1024]{1,0:T(8,128)(2,1)}, u32[]{:S(2)}) copy-start(bf16[64,1024]{1,0:T(8,128)(2,1)} %b_ref.1) | copy-start | bytes 393220
  2.4 0.9 %copy-start.4 = (s32[64,64]{1,0:T(8,128)S(1)}, s32[64,64]{1,0:T(8,128)}, u32[]{:S(2)}) copy-start(s32[64,64]{1,0:T(8,128)} %xe_ref.1) | copy-start | bytes 49156
  2.4 0.9 %copy-start.5 = (f32[2048]{0:T(1024)S(1)}, f32[2048]{0:T(1024)}, u32[]{:S(2)}) copy-start(f32[2048]{0:T(1024)} %param.24) | copy-start | bytes 24580
  2.4 0.9 %copy-start.6 = (f32[32]{0:T(128)S(1)}, f32[32]{0:T(128)}, u32[]{:S(2)}) copy-start(f32[32]{0:T(128)} %param.21) | copy-start | bytes 388
  2.4 0.9 %copy-start.7 = (f32[32]{0:T(128)S(1)}, f32[32]{0:T(128)}, u32[]{:S(2)}) copy-start(f32[32]{0:T(128)} %param.22) | copy-start | bytes 388
  2.4 0.9 %copy-start.8 = (s32[8]{0:T(128)S(1)}, s32[8]{0:T(128)}, u32[]{:S(2)}) copy-start(s32[8]{0:T(128)} %starts_ref.1) | copy-start | bytes 100
  3.4 1.2 %copy-start = (bf16[64,8192]{1,0:T(8,128)(2,1)S(1)}, bf16[64,8192]{1,0:T(8,128)(2,1)}, u32[]{:S(2)}) copy-start(bf16[64,8192]{1,0:T(8,128)(2,1)} %x_hbm.1) | copy-start | bytes 3145732
  4.6 1.2 %copy-start.1 = (bf16[256,2048]{1,0:T(8,128)(2,1)S(1)}, bf16[256,2048]{1,0:T(8,128)(2,1)}, u32[]{:S(2)}) copy-start(bf16[256,2048]{1,0:T(8,128)(2,1)} %z_hbm.1) | copy-start | bytes 3145732
  5.8 0.9 %copy-start.3 = (bf16[64,1024]{1,0:T(8,128)(2,1)S(1)}, bf16[64,1024]{1,0:T(8,128)(2,1)}, u32[]{:S(2)}) copy-start(bf16[64,1024]{1,0:T(8,128)(2,1)} %c_ref.1) | copy-start | bytes 393220

commit v2 on v1

v2 whole, which is shorter than its diff:
```python
import functools

import jax
import jax.numpy as jnp
from jax import lax
from jax.experimental import pallas as pl
from jax.experimental.pallas import tpu as pltpu
from jax.sharding import PartitionSpec as P

F32 = jnp.float32
BF16 = jnp.bfloat16
P_SIZE = 64
N = 128
SPAN = 128
QB = 128
EPS = 1e-05
NX, NZ, NC, NT = 4, 8, 2, 4
CUT = 2


def split3(v):
    hi = v.astype(BF16)
    rest = v - hi.astype(F32)
    mid = rest.astype(BF16)
    low = (rest - mid.astype(F32)).astype(BF16)
    return hi, mid, low


def dot(a, b):
    return jnp.dot(a, b, preferred_element_type=F32)


def kernel(
    x_hbm,
    xe_hbm,
    b_hbm,
    be_hbm,
    c_hbm,
    ce_hbm,
    z_hbm,
    dtr_hbm,
    bias_hbm,
    alog_hbm,
    skip_hbm,
    gain_hbm,
    starts_hbm,
    obuf,
    xs,
    xe_ref,
    bs,
    be_ref,
    cs,
    ce_ref,
    zbuf,
    dtr_ref,
    bias_ref,
    alog_ref,
    skip_ref,
    gain_ref,
    starts_ref,
    xbuf,
    bbuf,
    cbuf,
    turn_in,
    turned,
    tailx,
    reachx,
    rows_in,
    rows_ex,
    gsend,
    gpair,
    gz,
    gx,
    sfirst,
    sdev,
    sdev16,
    pairs,
    tot16,
    zbuf_in,
    prefix,
    xsend,
    xin,
    esend,
    ein,
    keep,
    psend,
    ent,
    cbm,
    acc,
    mixed,
    powers,
    load_sem,
    own_sem,
    y_send,
    y_recv,
    g_send,
    g_recv,
    p_send,
    p_recv,
    z_send,
    z_recv,
    l_send,
    l_recv,
):
    rows = xbuf.shape[0]
    slab = rows // NT
    heads = dtr_ref.shape[0]
    width = xbuf.shape[1]
    groups = bbuf.shape[1] // N
    per_group = heads // groups
    gw = width // groups
    cw = gw // CUT
    chunks = groups * CUT
    half = cw // NC
    zr = N // NZ
    blocks = rows // SPAN

    s = lax.axis_index("seq")
    t = lax.axis_index("tp")
    xx = s // (NZ * NC)
    zz = (s // NC) % NZ
    cc = s % NC
    mate = s + 1 - 2 * cc

    def y_dev(k):
        return {"seq": s, "tp": (t + k) % NT}

    def z_dev(k):
        return {"seq": xx * (NZ * NC) + ((zz + k) % NZ) * NC + cc, "tp": t}

    def x_dev(k):
        return {"seq": ((xx + k) % NX) * (NZ * NC) + zz * NC + cc, "tp": t}

    mate_dev = {"seq": mate, "tp": t}

    barrier = pltpu.get_barrier_semaphore()

    def greet(dev):
        pl.semaphore_signal(barrier, inc=1, device_id=dev, device_id_type=pl.DeviceIdType.MESH)

    def load(src, dst, k):
        copy = pltpu.make_async_copy(src, dst, load_sem.at[k])
        copy.start()
        return copy

    b_load = load(b_hbm, bs, 0)
    be_load = load(be_hbm, be_ref, 1)
    x_load = load(x_hbm, xs, 3)
    xe_load = load(xe_hbm, xe_ref, 2)

    def greet_loop(make):
        def one(k, _):
            greet(make(k))
            return 0

        return one

    lax.fori_loop(1, NT, greet_loop(y_dev), 0)
    lax.fori_loop(1, NZ, greet_loop(z_dev), 0)
    lax.fori_loop(1, NX, greet_loop(x_dev), 0)
    greet(mate_dev)
    small = [
        load(dtr_hbm, dtr_ref, 6),
        load(bias_hbm, bias_ref, 7),
        load(alog_hbm, alog_ref, 8),
        load(skip_hbm, skip_ref, 9),
        load(starts_hbm, starts_ref, 11),
    ]

    def remote(src, dst, send, recv, dev):
        return pltpu.make_async_remote_copy(
            src_ref=src,
            dst_ref=dst,
            send_sem=send,
            recv_sem=recv,
            device_id=dev,
            device_id_type=pl.DeviceIdType.MESH,
        )

    made = {}
    arrived = set()
    sent = set()

    def each(tag, what):
        count, make = made[tag]
        if count is None:
            getattr(make(0), what)()
            return

        def one(i, _):
            step = (i + 1) // 2
            getattr(make(count // 2 + step * (1 - 2 * (i % 2))), what)()
            return 0

        lax.fori_loop(0, count - 1, one, 0)

    def put(tag, count, make):
        made[tag] = (count, make)
        each(tag, "start")

    def got(tag):
        arrived.add(tag)
        each(tag, "wait_recv")

    def flush():
        for tag in made:
            if tag not in sent:
                each(tag, "wait_send")
                sent.add(tag)

    def y_copy(piece, k):
        to = (t + k) % NT
        mine = pl.ds(pl.multiple_of(t * slab, slab), slab)
        if piece == 0 or piece == chunks + 1:
            src, dst = (bs, bbuf) if piece == 0 else (cs, cbuf)
            w = groups * N
            src = src.at[:, pl.ds(pl.multiple_of(to * w, w), w)]
            dst = dst.at[mine, :]
        else:
            q = piece - 1
            src = xs.at[:, pl.ds(pl.multiple_of(to * width + q * cw, cw), cw)]
            dst = xbuf.at[mine, pl.ds(q * cw, cw)]
        return remote(src, dst, y_send.at[piece, k], y_recv.at[piece, k], y_dev(k))

    def y_own(piece):
        mine = pl.ds(pl.multiple_of(t * slab, slab), slab)
        if piece == 0 or piece == chunks + 1:
            src, dst = (bs, bbuf) if piece == 0 else (cs, cbuf)
            w = groups * N
            src = src.at[:, pl.ds(pl.multiple_of(t * w, w), w)]
            dst = dst.at[mine, :]
        else:
            q = piece - 1
            src = xs.at[:, pl.ds(pl.multiple_of(t * width + q * cw, cw), cw)]
            dst = xbuf.at[mine, pl.ds(q * cw, cw)]
        return pltpu.make_async_copy(src, dst, own_sem.at[piece])

    def y_start(piece):
        put(("y", piece), NT, functools.partial(y_copy, piece))
        y_own(piece).start()

    def y_wait(piece):
        got(("y", piece))
        y_own(piece).wait()

    def scale_cols(buf, exps, cols):
        for j in cols:
            at = slice(j * QB, (j + 1) * QB)
            buf[:, at] = (buf[:, at].astype(F32) * exps[:, j : j + 1]).astype(BF16)

    per_x = cw // QB

    def x_scale(q):
        cols = [d * chunks * per_x + q * per_x + j for d in range(NT) for j in range(per_x)]
        scale_cols(xs, jnp.exp2(xe_ref[...].astype(F32)), cols)

    def c_scale():
        scale_cols(cs, jnp.exp2(jnp.transpose(ce_ref[...].astype(F32))), range(NT * groups))

    b_load.wait()
    be_load.wait()
    scale_cols(bs, jnp.exp2(jnp.transpose(be_ref[...].astype(F32))), range(NT * groups))
    xe_load.wait()
    x_load.wait()
    x_scale(0)
    pl.semaphore_wait(barrier, (NT - 1) + (NZ - 1) + (NX - 1) + 1)
    y_start(0)
    y_start(1)
    late = [
        load(c_hbm, cs, 4),
        load(ce_hbm, ce_ref, 5),
        load(z_hbm, zbuf, 12),
        load(gain_hbm, gain_ref, 10),
    ]
    for copy in small:
        copy.wait()

    def document(position):
        total = jnp.zeros(position.shape, jnp.int32)
        for k in range(starts_ref.shape[0]):
            total = total + (starts_ref[k] <= position).astype(jnp.int32)
        return total

    first = s * rows
    row_i = lax.broadcasted_iota(jnp.int32, (SPAN, SPAN), 0)
    col_i = lax.broadcasted_iota(jnp.int32, (SPAN, SPAN), 1)
    one_row = jnp.zeros((1, SPAN), jnp.int32)

    def column(row):
        eye = row_i[:heads, :heads] == col_i[:heads, :heads]
        return jnp.sum(jnp.where(eye, row, 0.0), axis=1, keepdims=True)

    raw = dtr_ref[...].astype(F32) + column(bias_ref[...])
    step = jnp.maximum(raw, 0.0) + jnp.log1p(jnp.exp(-jnp.abs(raw)))
    rate = -step * jnp.exp(column(alog_ref[...]))
    tri = (row_i <= col_i).astype(BF16)
    lead = lax.broadcasted_iota(jnp.int32, (SPAN, width), 0)
    chan = lax.broadcasted_iota(jnp.int32, (SPAN, width), 1) // P_SIZE

    def grow(v, parts, shift):
        spread = (lead[: v.shape[1]] == chan[: v.shape[1]] + shift).astype(BF16)
        pieces = split3(v)[:parts]
        total = dot(pieces[0], spread)
        for piece in pieces[1:]:
            total = total + dot(piece, spread)
        return total

    turn_in[...] = jnp.zeros_like(turn_in)
    same = []
    gains = []
    for b in range(blocks):
        at = slice(b * SPAN, (b + 1) * SPAN)
        parts = split3(rate[:, at])
        cum = dot(parts[0], tri) + dot(parts[1], tri) + dot(parts[2], tri)
        base = first + b * SPAN
        doc_j = document(base + col_i[:1])
        same.append((document(base + row_i) == doc_j) & (row_i >= col_i))
        doc_last = document(base + SPAN - 1 + one_row)
        prior = document(base - 1 + one_row)
        last = cum[:, SPAN - 1 : SPAN]
        tail = jnp.where(doc_j == doc_last, jnp.exp(jnp.minimum(last - cum, 0.0)), 0.0)
        reach = jnp.where(doc_j == prior, jnp.exp(cum), 0.0)
        turn_in[b, :heads] = cum
        turn_in[b, heads : 2 * heads] = tail * step[:, at]
        turn_in[b, 2 * heads : 3 * heads] = reach
        turn_in[b, 3 * heads : 4 * heads] = step[:, at]
        turned[b] = jnp.transpose(turn_in[b])
        gains.append(
            jnp.where(
                doc_last[:, :heads] == prior[:, :heads],
                jnp.exp(turned[b, SPAN - 1 : SPAN, :heads]),
                0.0,
            )
        )

    gdev = gains[0]
    for b in range(1, blocks):
        gdev = gdev * gains[b]

    gsend[...] = jnp.zeros_like(gsend)
    gsend[0, 0:1, :heads] = gdev

    def pair_gain(_):
        return remote(gsend.at[0], gpair, g_send.at[0], g_recv.at[0], mate_dev)

    put("pg", None, pair_gain)

    def z_gain(k):
        return remote(gsend.at[1], gz.at[zz], g_send.at[k], g_recv.at[k], z_dev(k))

    def x_gain(k):
        return remote(
            gsend.at[2], gx.at[xx], g_send.at[NZ - 1 + k], g_recv.at[NZ - 1 + k], x_dev(k)
        )

    x_scale(1)
    y_start(2)
    rows_in[...] = jnp.zeros_like(rows_in)
    for b in range(blocks):
        rows_in[b : b + 1, :] = gains[b]
    rows_in[4:5, :] = skip_ref[...]
    for b in range(blocks):
        tailx[b * SPAN : (b + 1) * SPAN, :] = grow(turned[b], 2, heads)
    x_scale(2)
    y_start(3)
    x_scale(3)
    got("pg")
    gother = gpair[0:1, :heads]
    gfirst = jnp.where(cc == 0, gdev, gother)
    gsecond = jnp.where(cc == 0, gother, gdev)
    gsend[1, 0:1, :heads] = gfirst * gsecond
    gz[pl.ds(zz, 1)] = gsend[1:2]
    put("zg", NZ, z_gain)
    rows_in[2:3, :] = gfirst
    rows_in[3:4, :] = gsecond
    rows_ex[0:8] = grow(rows_in[0:8], 3, 0)
    for copy in late:
        copy.wait()
    c_scale()

    def line_gains():
        got("zg")
        gline = gz[0][0:1, :heads]
        before = [jnp.ones((1, heads), F32)]
        for k in range(1, NZ):
            before.append(gline)
            gline = gline * gz[k][0:1, :heads]
        gsend[2, 0:1, :heads] = gline
        gx[pl.ds(xx, 1)] = gsend[2:3]
        put("xg", NX, x_gain)
        for k in range(NZ):
            rows_in[8 + k : 9 + k, :] = gz[k][0:1, :heads]
            rows_in[16 + k : 17 + k, :] = before[k]
        rows_ex[8:24] = grow(rows_in[8:24], 3, 0)

    def far_gains():
        got("xg")
        for k in range(NX):
            rows_in[24 + k : 25 + k, :] = gx[k][0:1, :heads]
        rows_ex[24:32] = grow(rows_in[24:32], 3, 0)

    def gate():
        zf = zbuf[...].astype(F32)
        acc[...] = zf / (1.0 + jnp.exp(-zf))

    def reaches():
        for b in range(blocks):
            reachx[b * SPAN : (b + 1) * SPAN, :] = grow(turned[b], 2, 2 * heads)

    def my_half(q):
        return pl.ds(pl.multiple_of(q * cw + cc * half, half), half)

    def other_half(q):
        return pl.ds(pl.multiple_of(q * cw + (1 - cc) * half, half), half)

    def pair_copy(q, _):
        return remote(
            sdev16.at[:, other_half(q)], pairs.at[q], p_send.at[0, q], p_recv.at[0, q], mate_dev
        )

    def states(q):
        at = slice(q * cw, (q + 1) * cw)
        g = q // CUT
        state = None
        for b in range(blocks):
            ta = slice(b * SPAN, (b + 1) * SPAN)
            scaled = (tailx[ta, at] * xbuf[ta, at].astype(F32)).astype(BF16)
            bv = bbuf[ta, g * N : (g + 1) * N]
            block = lax.dot_general(
                bv, scaled, (((0,), (0,)), ((), ())), preferred_element_type=F32
            )
            if b == 0:
                sfirst[:, at] = block
                state = block
            else:
                state = rows_ex[b : b + 1, at] * state + block
        sdev[:, at] = state
        sdev16[:, at] = state.astype(BF16)
        put(("p", q), None, functools.partial(pair_copy, q))

    def z_copy(q, k):
        to = (zz + k) % NZ
        return remote(
            tot16.at[q, pl.ds(pl.multiple_of(to * zr, zr), zr), :],
            zbuf_in.at[q, zz],
            z_send.at[0, q, k],
            z_recv.at[0, q, k],
            z_dev(k),
        )

    def chip_total(q):
        got(("p", q))
        mine = sdev[:, my_half(q)]
        other = pairs[q].astype(F32)
        early = jnp.where(cc == 0, mine, other)
        late = jnp.where(cc == 0, other, mine)
        pairs_total = rows_ex[3:4, my_half(q)] * early + late
        keep[q] = early
        tot16[q] = pairs_total.astype(BF16)
        zbuf_in[q, pl.ds(zz, 1)] = tot16[q, pl.ds(pl.multiple_of(zz * zr, zr), zr), :][None]
        put(("z", q), NZ, functools.partial(z_copy, q))

    def x_copy(q, k):
        return remote(
            xsend.at[q], xin.at[q, xx], l_send.at[q, k], l_recv.at[q, k], x_dev(k)
        )

    def line_scan(q):
        got(("z", q))
        run = jnp.zeros((zr, half), F32)
        for k in range(NZ):
            prefix[q, k] = run
            run = rows_ex[8 + k : 9 + k, my_half(q)] * run + zbuf_in[q, k].astype(F32)
        xsend[q] = run
        xin[q, pl.ds(xx, 1)] = run[None]
        put(("x", q), NX, functools.partial(x_copy, q))

    def e_copy(q, k):
        to = (zz + k) % NZ
        return remote(
            esend.at[q, to],
            ein.at[q, pl.ds(pl.multiple_of(zz * zr, zr), zr), :],
            z_send.at[1, q, k],
            z_recv.at[1, q, k],
            z_dev(k),
        )

    def enter(q):
        got(("x", q))
        run = jnp.zeros((zr, half), F32)
        for k in range(NX):
            after = rows_ex[24 + k : 25 + k, my_half(q)] * run + xin[q, k]
            run = jnp.where(k < xx, after, run)
        for k in range(NZ):
            esend[q, k] = (prefix[q, k] + rows_ex[16 + k : 17 + k, my_half(q)] * run).astype(BF16)
        ein[q, pl.ds(pl.multiple_of(zz * zr, zr), zr), :] = esend[q, pl.ds(zz, 1)][0]
        put(("e", q), NZ, functools.partial(e_copy, q))

    def back_copy(q, _):
        return remote(
            psend.at[q], ent.at[:, my_half(q)], p_send.at[1, q], p_recv.at[1, q], mate_dev
        )

    def back(q):
        got(("e", q))
        at_first = ein[q].astype(F32)
        at_second = rows_ex[2:3, my_half(q)] * at_first + keep[q]
        psend[q] = jnp.where(cc == 0, at_second, at_first).astype(BF16)
        put(("b", q), None, functools.partial(back_copy, q))
        ent[:, my_half(q)] = jnp.where(cc == 0, at_first, at_second).astype(BF16)

    def inner(q):
        g = q // CUT
        lane = lax.broadcasted_iota(jnp.int32, (SPAN, 2 * P_SIZE), 1)

        def one(b, _):
            ta = pl.ds(pl.multiple_of(b * SPAN, SPAN), SPAN)
            cb = cbm[b, g]
            cums = turned[b]
            rows_t = turn_in[b]
            for pair in range(cw // (2 * P_SIZE)):
                cols = slice(q * cw + pair * 2 * P_SIZE, q * cw + (pair + 1) * 2 * P_SIZE)
                xp = xbuf[ta, cols]
                mixes = []
                first_head = q * (cw // P_SIZE) + 2 * pair
                for h in (first_head, first_head + 1):
                    gap = cums[:, h : h + 1] - rows_t[h : h + 1, :]
                    dt_row = rows_t[3 * heads + h : 3 * heads + h + 1, :]
                    mixes.append((cb * jnp.exp(jnp.minimum(gap, 0.0)) * dt_row).astype(BF16))
                left = jnp.where(lane < P_SIZE, xp, jnp.zeros_like(xp))
                right = jnp.where(lane < P_SIZE, jnp.zeros_like(xp), xp)
                y = dot(jnp.concatenate(mixes, axis=1), jnp.concatenate([left, right], axis=0))
                mixed[ta, cols] = y + rows_ex[4:5, cols] * xp.astype(F32)
            return 0

        lax.fori_loop(0, blocks, one, 0)

    def products():
        for b in range(blocks):
            ta = slice(b * SPAN, (b + 1) * SPAN)
            for g in range(groups):
                at = slice(g * N, (g + 1) * N)
                cb = lax.dot_general(
                    cbuf[ta, at], bbuf[ta, at], (((1,), (1,)), ((), ())), preferred_element_type=F32
                )
                cbm[b, g] = jnp.where(same[b], cb, 0.0)

    def finish(q):
        got(("b", q))
        at = slice(q * cw, (q + 1) * cw)
        g = q // CUT
        entering = ent[:, at]
        for b in range(blocks):
            ta = slice(b * SPAN, (b + 1) * SPAN)
            if b > 0:
                entering = (
                    rows_ex[b - 1 : b, at] * entering.astype(F32) + sfirst[:, at]
                ).astype(BF16)
            cv = cbuf[ta, g * N : (g + 1) * N]
            y = mixed[ta, at] + dot(cv, entering) * reachx[ta, at]
            gated = y * acc[ta, at]
            mixed[ta, at] = gated
            power = jnp.sum(gated * gated, axis=1, keepdims=True)
            powers[q, ta] = jnp.broadcast_to(power, (SPAN, 128))

    def norm(g):
        at = slice(g * gw, (g + 1) * gw)
        for b in range(blocks):
            ta = slice(b * SPAN, (b + 1) * SPAN)
            power = powers[g * CUT, ta]
            for k in range(1, CUT):
                power = power + powers[g * CUT + k, ta]
            factor = lax.rsqrt(power[:, 0:1] / gw + EPS)
            obuf[ta, at] = (mixed[ta, at] * factor * gain_ref[:, at]).astype(BF16)

    y_wait(0)
    y_wait(1)
    y_start(4)
    states(0)
    reaches()
    chip_total(0)
    gate()
    y_wait(2)
    states(1)
    line_gains()
    chip_total(1)
    y_wait(3)
    states(2)
    far_gains()
    chip_total(2)
    line_scan(0)
    line_scan(1)
    y_wait(4)
    y_start(chunks + 1)
    states(3)
    enter(0)
    chip_total(3)
    enter(1)
    line_scan(2)
    y_wait(chunks + 1)
    products()
    inner(0)
    inner(1)
    line_scan(3)
    enter(2)
    back(0)
    back(1)
    inner(2)
    enter(3)
    inner(3)
    finish(0)
    finish(1)
    norm(0)
    back(2)
    finish(2)
    flush()
    back(3)
    finish(3)
    norm(1)

    flush()


def body(
    x_codes,
    x_exps,
    b_codes,
    b_exps,
    c_codes,
    c_exps,
    z_gate,
    dt_raw,
    dt_bias,
    a_log,
    d_skip,
    norm_gain,
    doc_starts,
):
    rows, width = z_gate.shape
    slab = x_codes.shape[0]
    heads = dt_raw.shape[1]
    gn = b_codes.shape[1] // NT
    groups = gn // N
    gw = width // groups
    half = gw // CUT // NC
    chunks = groups * CUT
    zr = N // NZ
    blocks = rows // SPAN
    hbm = pl.BlockSpec(memory_space=pltpu.HBM)
    dma = pltpu.SemaphoreType.DMA
    return pl.pallas_call(
        kernel,
        out_shape=pltpu.VMEM((rows, width), BF16),
        in_specs=[hbm] * 13,
        out_specs=pl.BlockSpec(memory_space=pltpu.VMEM),
        scratch_shapes=[
            pltpu.VMEM(x_codes.shape, BF16),
            pltpu.VMEM(x_exps.shape, jnp.int32),
            pltpu.VMEM(b_codes.shape, BF16),
            pltpu.VMEM(b_exps.shape[::-1], jnp.int32),
            pltpu.VMEM(c_codes.shape, BF16),
            pltpu.VMEM(c_exps.shape[::-1], jnp.int32),
            pltpu.VMEM((rows, width), BF16),
            pltpu.VMEM((heads, rows), BF16),
            pltpu.VMEM((1, heads), F32),
            pltpu.VMEM((1, heads), F32),
            pltpu.VMEM((1, heads), F32),
            pltpu.VMEM((1, width), F32),
            pltpu.SMEM(doc_starts.shape, jnp.int32),
            pltpu.VMEM((rows, width), BF16),
            pltpu.VMEM((rows, gn), BF16),
            pltpu.VMEM((rows, gn), BF16),
            pltpu.VMEM((blocks, SPAN, SPAN), F32),
            pltpu.VMEM((blocks, SPAN, SPAN), F32),
            pltpu.VMEM((rows, width), F32),
            pltpu.VMEM((rows, width), F32),
            pltpu.VMEM((32, heads), F32),
            pltpu.VMEM((32, width), F32),
            pltpu.VMEM((3, 8, 128), F32),
            pltpu.VMEM((8, 128), F32),
            pltpu.VMEM((NZ, 8, 128), F32),
            pltpu.VMEM((NX, 8, 128), F32),
            pltpu.VMEM((N, width), F32),
            pltpu.VMEM((N, width), F32),
            pltpu.VMEM((N, width), BF16),
            pltpu.VMEM((chunks, N, half), BF16),
            pltpu.VMEM((chunks, N, half), BF16),
            pltpu.VMEM((chunks, NZ, zr, half), BF16),
            pltpu.VMEM((chunks, NZ, zr, half), F32),
            pltpu.VMEM((chunks, zr, half), F32),
            pltpu.VMEM((chunks, NX, zr, half), F32),
            pltpu.VMEM((chunks, NZ, zr, half), BF16),
            pltpu.VMEM((chunks, N, half), BF16),
            pltpu.VMEM((chunks, N, half), F32),
            pltpu.VMEM((chunks, N, half), BF16),
            pltpu.VMEM((N, width), BF16),
            pltpu.VMEM((blocks, groups, SPAN, SPAN), F32),
            pltpu.VMEM((rows, width), F32),
            pltpu.VMEM((rows, width), F32),
            pltpu.VMEM((chunks, rows, 128), F32),
            dma((13,)),
            dma((chunks + 2,)),
            dma((chunks + 2, NT)),
            dma((chunks + 2, NT)),
            dma((NZ + NX,)),
            dma((NZ + NX,)),
            dma((2, chunks)),
            dma((2, chunks)),
            dma((2, chunks, NZ)),
            dma((2, chunks, NZ)),
            dma((chunks, NX)),
            dma((chunks, NX)),
        ],
        compiler_params=pltpu.CompilerParams(
            collective_id=0, has_side_effects=True, vmem_limit_bytes=56 * 1024 * 1024
        ),
    )(
        *(
            pltpu.with_memory_space_constraint(v, pltpu.HBM)
            for v in (
                x_codes,
                x_exps,
                b_codes,
                b_exps.T,
                c_codes,
                c_exps.T,
                z_gate,
                dt_raw.T,
                dt_bias[None, :],
                a_log[None, :],
                d_skip[None, :],
                norm_gain[None, :],
                doc_starts,
            )
        )
    )


def solution(mesh):
    placed = (
        P(("seq", "tp"), None),
        P(("seq", "tp"), None),
        P(("seq", "tp"), None),
        P(("seq", "tp"), None),
        P(("seq", "tp"), None),
        P(("seq", "tp"), None),
        P("seq", "tp"),
        P("seq", "tp"),
        P("tp"),
        P("tp"),
        P("tp"),
        P("tp"),
        P(),
    )
    return jax.shard_map(
        body, mesh=mesh, in_specs=placed, out_specs=P("seq", "tp"), check_vma=False
    )
```

time: 62.8 us -> 48.6 us (0.77)
  Pallas kernels: 54.8 us -> 47.5 us
  local copies, waits for them, and re-layouts: 7.6 us -> 0.97 us
    pallas_call x1, Pallas kernels: 54.8 us -> 47.5 us  [body(): pl.pallas_call(kernel, out_shape=pltpu.VMEM((rows, width), BF16), in_spec...]
    unnamed x22 -> x1, local copies, waits for them, and re-layouts: 6.76 us -> 0.97 us
    broadcast_in_dim x1 -> x0, local copies, waits for them, and re-layouts: 0.76 us -> none  [body(): jnp.repeat(d_skip, P_SIZE)[None, :]]
where the time goes in v2:
time: 48.6 us; the launch traced here: 48.5 us
  Pallas kernels  47.5 us (98%)
  local copies, waits for them, and re-layouts  0.97 us (2%)
    pallas_call x1, Pallas kernels, body(): pl.pallas_call(kernel, out_shape=pltpu.VMEM((rows, width), BF16), in_spec...  47.5 us
    unnamed x1, local copies, waits for them, and re-layouts  0.97 us

profile of v2, /device:TPU:1, one launch (start us, length us, event | category | flops | bytes accessed | tf_op | source)
XLA Modules:
  0.0 48.5 jit_solution(12777549410364243705)
XLA Ops:
  0.0 47.5 %shard_map.127 = bf16[256,2048]{1,0:T(8,128)(2,1)S(1)} custom-call(bf16[64,8192]{1,0:T(8,128)(2,1)} %x_hbm.1, s32[64,64]{1,0:T(8,128)} %xe_hbm.1, bf16[64,1024]{1,0:T(8,128)(2,1)} %b_hbm.1, s32[8,64]{1,0:T(8,128)} %bitcast.9, bf16[64,1024]{1,0:T(8,128)(2,1)} %c_hbm.1, s32[8,64]{1,0:T(8,128)} %bitcast.10, bf16[256,2048]{1,0:T(8,128)(2,1)} %z_hbm.1, ...), custom_call_target="tpu_custom_call" | custom-call | tf_op jit(solution)/shard_map/pallas_call | solution.py:651
  47.5 1.0 %copy.15 = bf16[256,2048]{1,0:T(8,128)(2,1)} copy(bf16[256,2048]{1,0:T(8,128)(2,1)S(1)} %shard_map.127) | data formatting | bytes 2097152

commit v3 on v2

--- a/solution.py
+++ b/solution.py
@@ -145,7 +145,11 @@
 
     b_load = load(b_hbm, bs, 0)
     be_load = load(be_hbm, be_ref, 1)
-    x_load = load(x_hbm, xs, 3)
+    part = xs.shape[0] // NT
+    x_loads = []
+    for k in range(NT):
+        at = pl.ds(k * part, part)
+        x_loads.append(load(x_hbm.at[at, :], xs.at[at, :], 12 + k))
     xe_load = load(xe_hbm, xe_ref, 2)
 
     def greet_loop(make):
@@ -261,7 +265,8 @@
     be_load.wait()
     scale_cols(bs, jnp.exp2(jnp.transpose(be_ref[...].astype(F32))), range(NT * groups))
     xe_load.wait()
-    x_load.wait()
+    for copy in x_loads:
+        copy.wait()
     x_scale(0)
     pl.semaphore_wait(barrier, (NT - 1) + (NZ - 1) + (NX - 1) + 1)
     y_start(0)
@@ -269,7 +274,7 @@
     late = [
         load(c_hbm, cs, 4),
         load(ce_hbm, ce_ref, 5),
-        load(z_hbm, zbuf, 12),
+        load(z_hbm, zbuf, 3),
         load(gain_hbm, gain_ref, 10),
     ]
     for copy in small:
@@ -579,39 +584,39 @@
     states(0)
     reaches()
     chip_total(0)
-    gate()
     y_wait(2)
     states(1)
     line_gains()
     chip_total(1)
+    gate()
     y_wait(3)
     states(2)
     far_gains()
     chip_total(2)
     line_scan(0)
+    y_wait(4)
+    y_start(chunks+1)
+    states(3)
+    chip_total(3)
     line_scan(1)
-    y_wait(4)
-    y_start(chunks + 1)
-    states(3)
     enter(0)
-    chip_total(3)
-    enter(1)
     line_scan(2)
-    y_wait(chunks + 1)
+    y_wait(chunks+1)
     products()
     inner(0)
     inner(1)
+    enter(1)
     line_scan(3)
     enter(2)
+    inner(2)
+    inner(3)
+    enter(3)
     back(0)
     back(1)
-    inner(2)
-    enter(3)
-    inner(3)
+    back(2)
     finish(0)
     finish(1)
     norm(0)
-    back(2)
     finish(2)
     flush()
     back(3)
@@ -698,7 +703,7 @@
             pltpu.VMEM((rows, width), F32),
             pltpu.VMEM((rows, width), F32),
             pltpu.VMEM((chunks, rows, 128), F32),
-            dma((13,)),
+            dma((12 + NT,)),
             dma((chunks + 2,)),
             dma((chunks + 2, NT)),
             dma((chunks + 2, NT)),

time: 48.6 us -> 45.9 us (0.944)
  Pallas kernels: 47.5 us -> 44.9 us
    pallas_call x1, Pallas kernels: 47.5 us -> 44.9 us  [body(): pl.pallas_call(kernel, out_shape=pltpu.VMEM((rows, width), BF16), in_spec...]
where the time goes in v3:
time: 45.9 us; the launch traced here: 45.8 us
  Pallas kernels  44.9 us (98%)
  local copies, waits for them, and re-layouts  0.97 us (2%)
    pallas_call x1, Pallas kernels, body(): pl.pallas_call(kernel, out_shape=pltpu.VMEM((rows, width), BF16), in_spec...  44.9 us
    unnamed x1, local copies, waits for them, and re-layouts  0.97 us

profile of v3, /device:TPU:1, one launch (start us, length us, event | category | flops | bytes accessed | tf_op | source)
XLA Modules:
  0.0 45.8 jit_solution(657549882649021741)
XLA Ops:
  0.0 44.9 %shard_map.127 = bf16[256,2048]{1,0:T(8,128)(2,1)S(1)} custom-call(bf16[64,8192]{1,0:T(8,128)(2,1)} %x_hbm.1, s32[64,64]{1,0:T(8,128)} %xe_hbm.1, bf16[64,1024]{1,0:T(8,128)(2,1)} %b_hbm.1, s32[8,64]{1,0:T(8,128)} %bitcast.9, bf16[64,1024]{1,0:T(8,128)(2,1)} %c_hbm.1, s32[8,64]{1,0:T(8,128)} %bitcast.10, bf16[256,2048]{1,0:T(8,128)(2,1)} %z_hbm.1, ...), custom_call_target="tpu_custom_call" | custom-call | tf_op jit(solution)/shard_map/pallas_call | solution.py:656
  44.9 1.0 %copy.15 = bf16[256,2048]{1,0:T(8,128)(2,1)} copy(bf16[256,2048]{1,0:T(8,128)(2,1)S(1)} %shard_map.127) | data formatting | bytes 2097152

commit v4 on v3

--- a/solution.py
+++ b/solution.py
@@ -601,16 +601,16 @@
     line_scan(1)
     enter(0)
     line_scan(2)
+    line_scan(3)
+    enter(1)
+    enter(2)
     y_wait(chunks+1)
     products()
     inner(0)
     inner(1)
-    enter(1)
-    line_scan(3)
-    enter(2)
+    enter(3)
     inner(2)
     inner(3)
-    enter(3)
     back(0)
     back(1)
     back(2)

time: 45.9 us -> 45.8 us (level)
  no operation moved by 1% of the time
where the time goes in v4:
time: 45.8 us; the launch traced here: 45.7 us
  Pallas kernels  44.7 us (98%)
  local copies, waits for them, and re-layouts  0.97 us (2%)
    pallas_call x1, Pallas kernels, body(): pl.pallas_call(kernel, out_shape=pltpu.VMEM((rows, width), BF16), in_spec...  44.7 us
    unnamed x1, local copies, waits for them, and re-layouts  0.97 us

profile of v4, /device:TPU:1, one launch (start us, length us, event | category | flops | bytes accessed | tf_op | source)
XLA Modules:
  0.0 45.7 jit_solution(10032310627649641841)
XLA Ops:
  0.0 44.7 %shard_map.127 = bf16[256,2048]{1,0:T(8,128)(2,1)S(1)} custom-call(bf16[64,8192]{1,0:T(8,128)(2,1)} %x_hbm.1, s32[64,64]{1,0:T(8,128)} %xe_hbm.1, bf16[64,1024]{1,0:T(8,128)(2,1)} %b_hbm.1, s32[8,64]{1,0:T(8,128)} %bitcast.9, bf16[64,1024]{1,0:T(8,128)(2,1)} %c_hbm.1, s32[8,64]{1,0:T(8,128)} %bitcast.10, bf16[256,2048]{1,0:T(8,128)(2,1)} %z_hbm.1, ...), custom_call_target="tpu_custom_call" | custom-call | tf_op jit(solution)/shard_map/pallas_call | solution.py:656
  44.7 1.0 %copy.15 = bf16[256,2048]{1,0:T(8,128)(2,1)} copy(bf16[256,2048]{1,0:T(8,128)(2,1)S(1)} %shard_map.127) | data formatting | bytes 2097152

commit v5 on v4

--- a/solution.py
+++ b/solution.py
@@ -271,6 +271,8 @@
     pl.semaphore_wait(barrier, (NT - 1) + (NZ - 1) + (NX - 1) + 1)
     y_start(0)
     y_start(1)
+    x_scale(1)
+    y_start(2)
     late = [
         load(c_hbm, cs, 4),
         load(ce_hbm, ce_ref, 5),
@@ -358,8 +360,6 @@
             gsend.at[2], gx.at[xx], g_send.at[NZ - 1 + k], g_recv.at[NZ - 1 + k], x_dev(k)
         )
 
-    x_scale(1)
-    y_start(2)
     rows_in[...] = jnp.zeros_like(rows_in)
     for b in range(blocks):
         rows_in[b : b + 1, :] = gains[b]
@@ -369,6 +369,7 @@
     x_scale(2)
     y_start(3)
     x_scale(3)
+    y_start(4)
     got("pg")
     gother = gpair[0:1, :heads]
     gfirst = jnp.where(cc == 0, gdev, gother)
@@ -580,7 +581,6 @@
 
     y_wait(0)
     y_wait(1)
-    y_start(4)
     states(0)
     reaches()
     chip_total(0)

time: 45.8 us -> 45.8 us (level)
  no operation moved by 1% of the time
where the time goes in v5:
time: 45.8 us; the launch traced here: 45.7 us
  Pallas kernels  44.7 us (98%)
  local copies, waits for them, and re-layouts  0.97 us (2%)
    pallas_call x1, Pallas kernels, body(): pl.pallas_call(kernel, out_shape=pltpu.VMEM((rows, width), BF16), in_spec...  44.7 us
    unnamed x1, local copies, waits for them, and re-layouts  0.97 us

profile of v5, /device:TPU:1, one launch (start us, length us, event | category | flops | bytes accessed | tf_op | source)
XLA Modules:
  0.0 45.7 jit_solution(16335598337368295391)
XLA Ops:
  0.0 44.7 %shard_map.127 = bf16[256,2048]{1,0:T(8,128)(2,1)S(1)} custom-call(bf16[64,8192]{1,0:T(8,128)(2,1)} %x_hbm.1, s32[64,64]{1,0:T(8,128)} %xe_hbm.1, bf16[64,1024]{1,0:T(8,128)(2,1)} %b_hbm.1, s32[8,64]{1,0:T(8,128)} %bitcast.9, bf16[64,1024]{1,0:T(8,128)(2,1)} %c_hbm.1, s32[8,64]{1,0:T(8,128)} %bitcast.10, bf16[256,2048]{1,0:T(8,128)(2,1)} %z_hbm.1, ...), custom_call_target="tpu_custom_call" | custom-call | tf_op jit(solution)/shard_map/pallas_call | solution.py:656
  44.7 1.0 %copy.15 = bf16[256,2048]{1,0:T(8,128)(2,1)} copy(bf16[256,2048]{1,0:T(8,128)(2,1)S(1)} %shard_map.127) | data formatting | bytes 2097152

commit v6 on v4

--- a/solution.py
+++ b/solution.py
@@ -89,6 +89,7 @@
     acc,
     mixed,
     powers,
+    spreads,
     load_sem,
     own_sem,
     y_send,
@@ -261,6 +262,12 @@
     def c_scale():
         scale_cols(cs, jnp.exp2(jnp.transpose(ce_ref[...].astype(F32))), range(NT * groups))
 
+    lead = lax.broadcasted_iota(jnp.int32, (SPAN, width), 0)
+    chan = lax.broadcasted_iota(jnp.int32, (SPAN, width), 1) // P_SIZE
+    for k in range(3):
+        spreads[k] = (lead == chan + k * heads).astype(BF16)
+    turn_in[...] = jnp.zeros_like(turn_in)
+    rows_in[...] = jnp.zeros_like(rows_in)
     b_load.wait()
     be_load.wait()
     scale_cols(bs, jnp.exp2(jnp.transpose(be_ref[...].astype(F32))), range(NT * groups))
@@ -299,18 +306,15 @@
     step = jnp.maximum(raw, 0.0) + jnp.log1p(jnp.exp(-jnp.abs(raw)))
     rate = -step * jnp.exp(column(alog_ref[...]))
     tri = (row_i <= col_i).astype(BF16)
-    lead = lax.broadcasted_iota(jnp.int32, (SPAN, width), 0)
-    chan = lax.broadcasted_iota(jnp.int32, (SPAN, width), 1) // P_SIZE
 
     def grow(v, parts, shift):
-        spread = (lead[: v.shape[1]] == chan[: v.shape[1]] + shift).astype(BF16)
+        spread = spreads[shift // heads, : v.shape[1]]
         pieces = split3(v)[:parts]
         total = dot(pieces[0], spread)
         for piece in pieces[1:]:
             total = total + dot(piece, spread)
         return total
 
-    turn_in[...] = jnp.zeros_like(turn_in)
     same = []
     gains = []
     for b in range(blocks):
@@ -360,7 +364,6 @@
 
     x_scale(1)
     y_start(2)
-    rows_in[...] = jnp.zeros_like(rows_in)
     for b in range(blocks):
         rows_in[b : b + 1, :] = gains[b]
     rows_in[4:5, :] = skip_ref[...]
@@ -582,13 +585,11 @@
     y_wait(1)
     y_start(4)
     states(0)
-    reaches()
     chip_total(0)
     y_wait(2)
     states(1)
     line_gains()
     chip_total(1)
-    gate()
     y_wait(3)
     states(2)
     far_gains()
@@ -599,6 +600,8 @@
     states(3)
     chip_total(3)
     line_scan(1)
+    gate()
+    reaches()
     enter(0)
     line_scan(2)
     line_scan(3)
@@ -703,6 +706,7 @@
             pltpu.VMEM((rows, width), F32),
             pltpu.VMEM((rows, width), F32),
             pltpu.VMEM((chunks, rows, 128), F32),
+            pltpu.VMEM((3, SPAN, width), BF16),
             dma((12 + NT,)),
             dma((chunks + 2,)),
             dma((chunks + 2, NT)),

time: 45.8 us -> 45.7 us (level)
  no operation moved by 1% of the time
where the time goes in v6:
time: 45.7 us; the launch traced here: 45.6 us
  Pallas kernels  44.7 us (98%)
  local copies, waits for them, and re-layouts  0.97 us (2%)
    pallas_call x1, Pallas kernels, body(): pl.pallas_call(kernel, out_shape=pltpu.VMEM((rows, width), BF16), in_spec...  44.7 us
    unnamed x1, local copies, waits for them, and re-layouts  0.97 us

profile of v6, /device:TPU:1, one launch (start us, length us, event | category | flops | bytes accessed | tf_op | source)
XLA Modules:
  0.0 45.6 jit_solution(6801283605888001784)
XLA Ops:
  0.0 44.7 %shard_map.127 = bf16[256,2048]{1,0:T(8,128)(2,1)S(1)} custom-call(bf16[64,8192]{1,0:T(8,128)(2,1)} %x_hbm.1, s32[64,64]{1,0:T(8,128)} %xe_hbm.1, bf16[64,1024]{1,0:T(8,128)(2,1)} %b_hbm.1, s32[8,64]{1,0:T(8,128)} %bitcast.9, bf16[64,1024]{1,0:T(8,128)(2,1)} %c_hbm.1, s32[8,64]{1,0:T(8,128)} %bitcast.10, bf16[256,2048]{1,0:T(8,128)(2,1)} %z_hbm.1, ...), custom_call_target="tpu_custom_call" | custom-call | tf_op jit(solution)/shard_map/pallas_call | solution.py:659
  44.7 1.0 %copy.15 = bf16[256,2048]{1,0:T(8,128)(2,1)} copy(bf16[256,2048]{1,0:T(8,128)(2,1)S(1)} %shard_map.127) | data formatting | bytes 2097152
